TPU v7x, 32 devices: a whole 2x2x4 slice. The times are simulated.
32 devices in a mesh: seq: 8 (over z, x), head: 4 (over y, core).
Axes of the slice: x: 2, y: 2, z: 4, core: 2. Of those that a mesh axis runs over, the one named last changes fastest.
Arguments:
- tokens: bfloat16 [2048, 4096], P('seq'), may hold values from -6 to 6
- w_query: bfloat16 [4096, 4096], P('seq', 'head'), may hold values from -0.09375 to 0.09375
- w_key: bfloat16 [4096, 4096], P('seq', 'head'), may hold values from -0.09375 to 0.09375
- w_value: bfloat16 [4096, 4096], P('seq', 'head'), may hold values from -0.09375 to 0.09375
- grad_out: bfloat16 [2048, 4096], P('seq', 'head'), may hold values from -6 to 6
Outputs:
- attn_out: bfloat16 [2048, 4096], P('seq', 'head')
- grad_x: bfloat16 [2048, 4096], P('seq', 'head')
- grad_wq: bfloat16 [4096, 4096], P('seq', 'head')
- grad_wk: bfloat16 [4096, 4096], P('seq', 'head')
- grad_wv: bfloat16 [4096, 4096], P('seq', 'head')
All inputs are finite; a program needn't handle non-finite values.
Results may differ from a plain program's by a relative error of at most 0.017.
Values may be sent and summed in bfloat16 or wider, within the bound.
A program may use at most 192 MiB of HBM per device.

v0:
```python
import math

import jax
import jax.numpy as jnp
from jax import lax
from jax.sharding import PartitionSpec as P

HD = 128
BLOCK = 128


def prefix(value, axis, join, neutral, backward):
    count = lax.axis_size(axis)
    place = lax.axis_index(axis)
    ahead = count - 1 - place if backward else place
    gathered = lax.all_gather(value.astype(jnp.bfloat16), axis)
    state = jnp.zeros_like(value) + jnp.asarray(neutral, value.dtype)

    def one(lap, state):
        source = count - 1 - lap if backward else lap
        return join(state, lax.dynamic_index_in_dim(gathered, source, 0, False).astype(value.dtype))

    return lax.fori_loop(0, ahead, one, state)


def add_states(earlier, later):
    return jax.tree.map(jnp.add, earlier, later)


def split_blocks(matrix, head_count):
    return matrix.reshape(matrix.shape[0] // BLOCK, BLOCK, head_count, HD)


def before_blocks(blocks, carried):
    running = jnp.cumsum(blocks, axis=0)
    return carried[None] + jnp.concatenate([jnp.zeros_like(blocks[:1]), running[:-1]], axis=0)


def after_blocks(blocks, carried):
    running = jnp.cumsum(blocks[::-1], axis=0)[::-1]
    return carried[None] + jnp.concatenate([running[1:], jnp.zeros_like(blocks[:1])], axis=0)


def per_device(tokens, w_query, w_key, w_value, grad_out):
    tok_rows = tokens.shape[0]
    col_count = w_query.shape[1]
    head_count = col_count // HD
    seq_count = lax.axis_size("seq")
    score_scale = 1.0 / math.sqrt(HD * tok_rows * seq_count)
    full_query, full_key, full_value = (
        lax.all_gather(w_query, "seq", axis=0, tiled=True),
        lax.all_gather(w_key, "seq", axis=0, tiled=True),
        lax.all_gather(w_value, "seq", axis=0, tiled=True),
    )
    queries = jnp.dot(tokens, full_query, preferred_element_type=jnp.float32).astype(jnp.bfloat16)
    keys_all = jnp.dot(tokens, full_key, preferred_element_type=jnp.float32).astype(jnp.bfloat16)
    values_all = jnp.dot(tokens, full_value, preferred_element_type=jnp.float32).astype(
        jnp.bfloat16
    )
    q_blocks = split_blocks(queries, head_count)
    k_blocks = split_blocks(keys_all, head_count)
    v_blocks = split_blocks(values_all, head_count)
    g_blocks = split_blocks(grad_out, head_count)
    kv_blocks = jnp.einsum(
        "bthd,bthe->bhde", k_blocks, v_blocks, preferred_element_type=jnp.float32
    )
    qg_blocks = jnp.einsum(
        "bthd,bthe->bhde", q_blocks, g_blocks, preferred_element_type=jnp.float32
    )
    kv_local = jnp.sum(kv_blocks, axis=0)
    qg_local = jnp.sum(qg_blocks, axis=0)
    zero_state = jnp.zeros_like(kv_local)
    kv_before = prefix(kv_local, "seq", add_states, zero_state, False)
    qg_after = prefix(qg_local, "seq", add_states, zero_state, True)
    prefix_state = before_blocks(kv_blocks, kv_before).astype(jnp.bfloat16)
    suffix_state = after_blocks(qg_blocks, qg_after).astype(jnp.bfloat16)
    causal_mask = lax.broadcasted_iota(jnp.int32, (BLOCK, BLOCK), 0) >= lax.broadcasted_iota(
        jnp.int32, (BLOCK, BLOCK), 1
    )
    raw_scores = jnp.einsum(
        "bthd,bshd->bhts", q_blocks, k_blocks, preferred_element_type=jnp.float32
    )
    scores = jnp.where(causal_mask, raw_scores * score_scale, 0.0).astype(jnp.bfloat16)
    intra = jnp.einsum("bhts,bshe->bthe", scores, v_blocks, preferred_element_type=jnp.float32)
    carried = jnp.einsum(
        "bthd,bhde->bthe", q_blocks, prefix_state, preferred_element_type=jnp.float32
    )
    attn_out = (intra + score_scale * carried).astype(jnp.bfloat16).reshape(tok_rows, col_count)
    raw_grad = jnp.einsum("bthe,bshe->bhts", g_blocks, v_blocks, preferred_element_type=jnp.float32)
    grad_scores = jnp.where(causal_mask, raw_grad * score_scale, 0.0).astype(jnp.bfloat16)
    grad_q = jnp.einsum(
        "bhts,bshd->bthd", grad_scores, k_blocks, preferred_element_type=jnp.float32
    ) + score_scale * jnp.einsum(
        "bthe,bhde->bthd", g_blocks, prefix_state, preferred_element_type=jnp.float32
    )
    grad_k = jnp.einsum(
        "bhts,bthd->bshd", grad_scores, q_blocks, preferred_element_type=jnp.float32
    ) + score_scale * jnp.einsum(
        "bshe,bhde->bshd", v_blocks, suffix_state, preferred_element_type=jnp.float32
    )
    grad_v = jnp.einsum(
        "bhts,bthe->bshe", scores, g_blocks, preferred_element_type=jnp.float32
    ) + score_scale * jnp.einsum(
        "bshd,bhde->bshe", k_blocks, suffix_state, preferred_element_type=jnp.float32
    )
    grad_q = grad_q.astype(jnp.bfloat16).reshape(tok_rows, col_count)
    grad_k = grad_k.astype(jnp.bfloat16).reshape(tok_rows, col_count)
    grad_v = grad_v.astype(jnp.bfloat16).reshape(tok_rows, col_count)
    partial_input = jnp.einsum("tc,dc->td", grad_q, full_query, preferred_element_type=jnp.float32)
    partial_input = partial_input + jnp.einsum(
        "tc,dc->td", grad_k, full_key, preferred_element_type=jnp.float32
    )
    partial_input = partial_input + jnp.einsum(
        "tc,dc->td", grad_v, full_value, preferred_element_type=jnp.float32
    )
    grad_x = lax.psum_scatter(
        partial_input.astype(jnp.bfloat16), "head", scatter_dimension=1, tiled=True
    )
    term_query = jnp.einsum("td,tc->dc", tokens, grad_q, preferred_element_type=jnp.float32)
    term_key = jnp.einsum("td,tc->dc", tokens, grad_k, preferred_element_type=jnp.float32)
    term_value = jnp.einsum("td,tc->dc", tokens, grad_v, preferred_element_type=jnp.float32)
    sum_query, sum_key, sum_value = (
        lax.psum_scatter(
            term_query.astype(jnp.bfloat16), "seq", scatter_dimension=0, tiled=True
        ).astype(jnp.float32),
        lax.psum_scatter(
            term_key.astype(jnp.bfloat16), "seq", scatter_dimension=0, tiled=True
        ).astype(jnp.float32),
        lax.psum_scatter(
            term_value.astype(jnp.bfloat16), "seq", scatter_dimension=0, tiled=True
        ).astype(jnp.float32),
    )
    grad_wq = sum_query.astype(jnp.bfloat16)
    grad_wk = sum_key.astype(jnp.bfloat16)
    grad_wv = sum_value.astype(jnp.bfloat16)
    return (attn_out, grad_x, grad_wq, grad_wk, grad_wv)


def solution(mesh):
    in_specs = (
        P("seq", None),
        P("seq", "head"),
        P("seq", "head"),
        P("seq", "head"),
        P("seq", "head"),
    )
    out_specs = (
        P("seq", "head"),
        P("seq", "head"),
        P("seq", "head"),
        P("seq", "head"),
        P("seq", "head"),
    )
    return jax.shard_map(
        per_device, mesh=mesh, in_specs=in_specs, out_specs=out_specs, check_vma=False
    )
```

profile of v0, /device:TPU:0, one launch (start us, length us, event | category | flops | bytes accessed | tf_op | source)
XLA Modules:
  0.0 984.1 jit_solution(1383071028200723850)
XLA Ops:
  9.4 128.4 %all-gather.12.cloned.1.call-done = bf16[4096,1024]{1,0:T(8,128)(2,1)} async-done(((bf16[512,1024]{1,0:T(8,128)(2,1)}), bf16[4096,1024]{1,0:T(8,128)(2,1)}) %all-gather.12.cloned.1.call-update) | async-done | bytes 8388624 | tf_op jit(solution)/shard_map/all_gather | solution.py:52
  137.8 5.7 fusion.17
  144.0 119.1 %all-gather.8.cloned.1.call-done = bf16[4096,1024]{1,0:T(8,128)(2,1)} async-done(((bf16[512,1024]{1,0:T(8,128)(2,1)}), bf16[4096,1024]{1,0:T(8,128)(2,1)}) %all-gather.8.cloned.1.call-update) | async-done | bytes 8388624 | tf_op jit(solution)/shard_map/all_gather | solution.py:53
  263.1 5.7 fusion.15
  268.9 2.0 fusion.49
  271.0 2.0 copy.126
  273.0 115.3 %all-gather.10.cloned.1.call-done = bf16[4096,1024]{1,0:T(8,128)(2,1)} async-done(((bf16[512,1024]{1,0:T(8,128)(2,1)}), bf16[4096,1024]{1,0:T(8,128)(2,1)}) %all-gather.10.cloned.1.call-update) | async-done | bytes 8388624 | tf_op jit(solution)/shard_map/all_gather | solution.py:51
  388.3 5.7 fusion.16
  396.4 3.2 fusion.50
  401.9 1.5 fusion.12
  405.8 32.2 %all-gather.14.cloned.1.call-done = bf16[64,128,128]{2,1,0:T(8,128)(2,1)} async-done(((bf16[8,128,128]{2,1,0:T(8,128)(2,1)}), bf16[64,128,128]{2,1,0:T(8,128)(2,1)}) %all-gather.14.cloned.1.call-update) | async-done | bytes 2097168 | tf_op jit(solution)/shard_map/all_gather | solution.py:16
  438.1 2.0 fusion.20
  441.2 5.6 convert_bitcast_fusion.2
  446.9 2.3 rev.4
  449.2 2.5 fusion.53
  451.8 36.0 %all-gather.16.cloned.1.call-done = bf16[64,128,128]{2,1,0:T(8,128)(2,1)} async-done(((bf16[8,128,128]{2,1,0:T(8,128)(2,1)}), bf16[64,128,128]{2,1,0:T(8,128)(2,1)}) %all-gather.16.cloned.1.call-update) | async-done | bytes 2097168 | tf_op jit(solution)/shard_map/all_gather | solution.py:16
  487.8 7.8 while.23
  498.0 1.9 fusion.19
  501.0 5.6 convert_bitcast_fusion.1
  507.7 1.6 fusion.13
  513.0 5.6 convert_bitcast_fusion
  519.6 5.9 fusion.27
  525.6 6.1 convolution_add_fusion.1
  531.7 7.5 fusion
  539.2 1.6 convolution_multiply_fusion.1
  543.4 95.9 %reduce-scatter.7.cloned.1.call-done = bf16[512,1024]{0,1:T(8,128)(2,1)} async-done(((bf16[4096,1024]{0,1:T(8,128)(2,1)}), bf16[512,1024]{0,1:T(8,128)(2,1)}) %reduce-scatter.7.cloned.1.call-update) | async-done | bytes 1048592 | tf_op jit(solution)/shard_map/reduce_scatter | solution.py:123
  639.3 2.3 copy.108
  641.5 150.2 %reduce-scatter.9.cloned.1.call-done = bf16[512,1024]{0,1:T(8,128)(2,1)} async-done(((bf16[4096,1024]{0,1:T(8,128)(2,1)}), bf16[512,1024]{0,1:T(8,128)(2,1)}) %reduce-scatter.9.cloned.1.call-update) | async-done | bytes 1048592 | tf_op jit(solution)/shard_map/reduce_scatter | solution.py:126
  791.8 2.3 copy.109
  794.0 149.8 %reduce-scatter.11.cloned.1.call-done = bf16[512,1024]{0,1:T(8,128)(2,1)} async-done(((bf16[4096,1024]{0,1:T(8,128)(2,1)}), bf16[512,1024]{0,1:T(8,128)(2,1)}) %reduce-scatter.11.cloned.1.call-update) | async-done | bytes 1048592 | tf_op jit(solution)/shard_map/reduce_scatter | solution.py:129
  943.8 2.3 copy.110
  946.1 31.5 %reduce-scatter.5.cloned.1.call-done = bf16[256,1024]{1,0:T(8,128)(2,1)} async-done(((bf16[256,4096]{1,0:T(8,128)(2,1)}), bf16[256,1024]{1,0:T(8,128)(2,1)}) %reduce-scatter.5.cloned.1.call-update) | async-done | bytes 524304 | tf_op jit(solution)/shard_map/reduce_scatter | solution.py:116
  (86 shorter events, 30.2 us)
Async XLA Ops:
  7.2 130.6 %copy-start = (bf16[256,4096]{1,0:T(8,128)(2,1)S(1)}, bf16[256,4096]{1,0:T(8,128)(2,1)}, u32[]{:S(2)}) copy-start(bf16[256,4096]{1,0:T(8,128)(2,1)} %param.9) | copy-start | bytes 6291460
  7.2 130.6 %all-gather.12.cloned.1.call-start = ((), (), s32[]{:S(2)}) async-start(), calls=%async_computation.6 | async-start | bytes 9437184 | tf_op jit(solution)/shard_map/all_gather | solution.py:52
  7.9 255.2 %all-gather.8.cloned.1.call-start = ((), (), s32[]{:S(2)}) async-start(), calls=%async_computation.4 | async-start | bytes 9437184 | tf_op jit(solution)/shard_map/all_gather | solution.py:53
  8.7 379.7 %all-gather.10.cloned.1.call-start = ((), (), s32[]{:S(2)}) async-start(), calls=%async_computation.5 | async-start | bytes 9437184 | tf_op jit(solution)/shard_map/all_gather | solution.py:51
  9.4 428.6 %all-gather.14.cloned.1.call-start = ((), (), s32[]{:S(2)}) async-start(), calls=%async_computation.11 | async-start | bytes 2359296 | tf_op jit(solution)/shard_map/all_gather | solution.py:16
  143.6 119.5 %copy-start.7 = (bf16[32,8,8,128]{3,2,1,0:T(8,128)(2,1)}, bf16[32,8,8,128]{3,2,1,0:T(8,128)(2,1)S(1)}, u32[]{:S(2)}) copy-start(bf16[32,8,8,128]{3,2,1,0:T(8,128)(2,1)S(1)} %copy.123) | copy-start | bytes 1572868
  144.0 124.9 %copy-start.9 = (bf16[2,128,8,128]{1,3,2,0:T(8,128)(2,1)}, bf16[2,128,8,128]{1,3,2,0:T(8,128)(2,1)S(1)}, u32[]{:S(2)}) copy-start(bf16[2,128,8,128]{1,3,2,0:T(8,128)(2,1)S(1)} %copy.80) | copy-start | bytes 1572868
  268.9 133.1 %copy-start.1 = (bf16[32,8,8,128]{3,2,1,0:T(8,128)(2,1)}, bf16[32,8,8,128]{3,2,1,0:T(8,128)(2,1)S(1)}, u32[]{:S(2)}) copy-start(bf16[32,8,8,128]{3,2,1,0:T(8,128)(2,1)S(1)} %copy.124) | copy-start | bytes 1572868
  271.0 216.8 %all-gather.16.cloned.1.call-start = ((), (), s32[]{:S(2)}) async-start(), calls=%async_computation.12 | async-start | bytes 2359296 | tf_op jit(solution)/shard_map/all_gather | solution.py:16
  396.4 52.9 %copy-start.3 = (bf16[2,128,8,128]{1,3,2,0:T(8,128)(2,1)}, bf16[2,128,8,128]{1,3,2,0:T(8,128)(2,1)S(1)}, u32[]{:S(2)}) copy-start(bf16[2,128,8,128]{1,3,2,0:T(8,128)(2,1)S(1)} %copy.95) | copy-start | bytes 1572868
  399.6 239.6 %reduce-scatter.7.cloned.1.call-start = ((), (), s32[]{:S(2)}) async-start(), calls=%async_computation.8 | async-start | bytes 9437184 | tf_op jit(solution)/shard_map/reduce_scatter | solution.py:123
  399.7 4.6 copy-start.10
  403.5 0.8 copy-start.12
  440.4 0.8 copy-start.13
  446.9 344.9 %reduce-scatter.9.cloned.1.call-start = ((), (), s32[]{:S(2)}) async-start(), calls=%async_computation.9 | async-start | bytes 9437184 | tf_op jit(solution)/shard_map/reduce_scatter | solution.py:126
  449.2 46.4 %copy-start.19 = (pred[2]{0:T(512)(128)(4,1)S(1)}, pred[2]{0:T(512)(128)(4,1)}, u32[]{:S(2)}) copy-start(pred[2]{0:T(512)(128)(4,1)} %constant.54.clone.1) | copy-start | bytes 10
  497.2 0.8 copy-start.5
  500.2 0.8 copy-start.15
  506.6 1.0 copy-start.4
  506.6 437.2 %reduce-scatter.11.cloned.1.call-start = ((), (), s32[]{:S(2)}) async-start(), calls=%async_computation.10 | async-start | bytes 9437184 | tf_op jit(solution)/shard_map/reduce_scatter | solution.py:129
  507.7 3.9 copy-start.6
  507.7 3.9 copy-start.8
  509.3 0.8 copy-start.11
  512.2 0.8 copy-start.17
  518.6 1.0 copy-start.14
  518.6 458.9 %reduce-scatter.5.cloned.1.call-start = ((), (), s32[]{:S(2)}) async-start(), calls=%async_computation.7 | async-start | bytes 2621440 | tf_op jit(solution)/shard_map/reduce_scatter | solution.py:116
  519.6 5.9 copy-start.16
  525.6 6.1 copy-start.18
  539.2 1.6 copy-start.2
Sparse Core Ops, SparseCore 0:
  10.1 127.6 all-gather.11
  139.9 123.1 all-gather.7
  265.2 123.1 all-gather.9
  390.3 47.6 all-gather.13
  440.0 47.7 all-gather.15
  491.3 147.9 reduce-scatter.6
  643.3 148.3 reduce-scatter.8
  795.4 148.3 reduce-scatter.10
  947.1 30.4 reduce-scatter.4
where the time goes:
time: 985 us; the launch traced here: 984 us
  waiting for transfers between devices  860 us (87%)
  matrix products  74.4 us (8%)
  local copies, waits for them, and re-layouts  23.7 us (2%)
  between operations  14.2 us (1%)
  other arithmetic  10.3 us (1%)
    reduce_scatter x1, waiting for transfers between devices, per_device(): lax.psum_scatter(term_key.astype(jnp.bfloat16), 'seq', scatter_dimension=...  150 us
    reduce_scatter x1, waiting for transfers between devices, per_device(): lax.psum_scatter(term_value.astype(jnp.bfloat16), 'seq', scatter_dimensio...  150 us
    all_gather x1, waiting for transfers between devices, per_device(): lax.all_gather(w_key, 'seq', axis=0, tiled=True)  128 us
    all_gather x1, waiting for transfers between devices, per_device(): lax.all_gather(w_value, 'seq', axis=0, tiled=True)  119 us
    all_gather x1, waiting for transfers between devices, per_device(): lax.all_gather(w_query, 'seq', axis=0, tiled=True)  115 us
    reduce_scatter x1, waiting for transfers between devices, per_device(): lax.psum_scatter(term_query.astype(jnp.bfloat16), 'seq', scatter_dimensio...  95.9 us
    all_gather x2, waiting for transfers between devices, prefix(): gathered = lax.all_gather(value.astype(jnp.bfloat16), axis)  68.2 us
    reduce_scatter x1, waiting for transfers between devices, per_device(): lax.psum_scatter(partial_input.astype(jnp.bfloat16), 'head', scatter_dime...  31.5 us
  transfers between devices with their start and end apart: 9, of which 9 were waited for; matrix products, arithmetic and copies ran while one was open for 10% of the time, Pallas kernels for 0%

commit v1 on v0

--- a/solution.py
+++ b/solution.py
@@ -136,6 +136,94 @@
     return (attn_out, grad_x, grad_wq, grad_wk, grad_wv)
 
 
+def head_attention(queries, keys, values, grads, score_scale):
+    head_count = queries.shape[1] // HD
+    q_blocks = split_blocks(queries, head_count)
+    k_blocks = split_blocks(keys, head_count)
+    v_blocks = split_blocks(values, head_count)
+    g_blocks = split_blocks(grads, head_count)
+    f32 = jnp.float32
+    kv_blocks = jnp.einsum("bthd,bthe->bhde", k_blocks, v_blocks, preferred_element_type=f32)
+    qg_blocks = jnp.einsum("bthd,bthe->bhde", q_blocks, g_blocks, preferred_element_type=f32)
+    zero_state = jnp.zeros_like(kv_blocks[0])
+    prefix_state = before_blocks(kv_blocks, zero_state).astype(jnp.bfloat16)
+    suffix_state = after_blocks(qg_blocks, zero_state).astype(jnp.bfloat16)
+    causal_mask = lax.broadcasted_iota(jnp.int32, (BLOCK, BLOCK), 0) >= lax.broadcasted_iota(
+        jnp.int32, (BLOCK, BLOCK), 1
+    )
+    raw_scores = jnp.einsum("bthd,bshd->bhts", q_blocks, k_blocks, preferred_element_type=f32)
+    scores = jnp.where(causal_mask, raw_scores * score_scale, 0.0).astype(jnp.bfloat16)
+    raw_grad = jnp.einsum("bthe,bshe->bhts", g_blocks, v_blocks, preferred_element_type=f32)
+    grad_scores = jnp.where(causal_mask, raw_grad * score_scale, 0.0).astype(jnp.bfloat16)
+
+    def close(within, across):
+        return (within + score_scale * across).astype(jnp.bfloat16).reshape(queries.shape)
+
+    attn_out = close(
+        jnp.einsum("bhts,bshe->bthe", scores, v_blocks, preferred_element_type=f32),
+        jnp.einsum("bthd,bhde->bthe", q_blocks, prefix_state, preferred_element_type=f32),
+    )
+    grad_q = close(
+        jnp.einsum("bhts,bshd->bthd", grad_scores, k_blocks, preferred_element_type=f32),
+        jnp.einsum("bthe,bhde->bthd", g_blocks, prefix_state, preferred_element_type=f32),
+    )
+    grad_k = close(
+        jnp.einsum("bhts,bthd->bshd", grad_scores, q_blocks, preferred_element_type=f32),
+        jnp.einsum("bshe,bhde->bshd", v_blocks, suffix_state, preferred_element_type=f32),
+    )
+    grad_v = close(
+        jnp.einsum("bhts,bthe->bshe", scores, g_blocks, preferred_element_type=f32),
+        jnp.einsum("bshd,bhde->bshe", k_blocks, suffix_state, preferred_element_type=f32),
+    )
+    return attn_out, grad_q, grad_k, grad_v
+
+
+def columns_first(matrix, parts):
+    return jnp.transpose(matrix.reshape(matrix.shape[0], parts, -1), (1, 0, 2))
+
+
+def columns_last(pieces):
+    return jnp.transpose(pieces, (1, 0, 2)).reshape(pieces.shape[1], -1)
+
+
+def per_head(tokens, w_query, w_key, w_value, grad_out):
+    seq_count, head_axis = lax.axis_size("seq"), lax.axis_size("head")
+    tok_rows, width = tokens.shape
+    weight_rows, col_count = w_query.shape
+    own = col_count // seq_count
+    score_scale = 1.0 / math.sqrt(HD * tok_rows * seq_count)
+    share = tok_rows // head_axis
+    mine = lax.dynamic_slice_in_dim(tokens, lax.axis_index("head") * share, share, 0)
+    every = lax.all_gather(mine, ("seq", "head"), axis=0, tiled=True)
+    weights = jnp.concatenate(
+        [columns_first(w, seq_count) for w in (w_query, w_key, w_value)], axis=2
+    )
+    weights = lax.all_to_all(weights, "seq", 0, 0, tiled=True).reshape(width, 3 * own)
+    grads = lax.all_to_all(columns_first(grad_out, seq_count), "seq", 0, 0, tiled=True)
+    grads = grads.reshape(tok_rows * seq_count, own)
+    projected = jnp.dot(every, weights, preferred_element_type=jnp.float32).astype(jnp.bfloat16)
+    attn_out, grad_q, grad_k, grad_v = head_attention(
+        projected[:, :own], projected[:, own : 2 * own], projected[:, 2 * own :], grads, score_scale
+    )
+    attn_out = columns_last(
+        lax.all_to_all(attn_out.reshape(seq_count, tok_rows, own), "seq", 0, 0, tiled=True)
+    )
+    gradient = jnp.concatenate([grad_q, grad_k, grad_v], axis=1)
+    partial_input = jnp.einsum("tc,dc->td", gradient, weights, preferred_element_type=jnp.float32)
+    grad_x = lax.psum_scatter(
+        partial_input.astype(jnp.bfloat16), "head", scatter_dimension=1, tiled=True
+    )
+    grad_x = lax.psum_scatter(grad_x, "seq", scatter_dimension=0, tiled=True)
+    grad_w = jnp.einsum("td,tc->dc", every, gradient, preferred_element_type=jnp.float32)
+    grad_w = lax.all_to_all(
+        grad_w.astype(jnp.bfloat16).reshape(seq_count, weight_rows, 3 * own), "seq", 0, 0, tiled=True
+    )
+    grad_wq, grad_wk, grad_wv = (
+        columns_last(grad_w[:, :, i * own : (i + 1) * own]) for i in range(3)
+    )
+    return (attn_out, grad_x, grad_wq, grad_wk, grad_wv)
+
+
 def solution(mesh):
     in_specs = (
         P("seq", None),
@@ -151,6 +239,16 @@
         P("seq", "head"),
         P("seq", "head"),
     )
-    return jax.shard_map(
-        per_device, mesh=mesh, in_specs=in_specs, out_specs=out_specs, check_vma=False
-    )
+
+    def whole(tokens, w_query, w_key, w_value, grad_out):
+        seq_count, head_axis = mesh.shape["seq"], mesh.shape["head"]
+        heads = w_query.shape[1] // HD
+        even = heads % (seq_count * head_axis) == 0 and tokens.shape[0] % (seq_count * head_axis) == 0
+        return mapped(per_head if even else per_device)(tokens, w_query, w_key, w_value, grad_out)
+
+    def mapped(body):
+        return jax.shard_map(
+            body, mesh=mesh, in_specs=in_specs, out_specs=out_specs, check_vma=False
+        )
+
+    return whole

time: 985 us -> 513 us (0.52)
  waiting for transfers between devices: 860 us -> 399 us
  matrix products: 74.4 us -> 52.3 us
  starting transfers between devices: 0.58 us -> 20.7 us
    all_gather x5 -> x1, waiting for transfers between devices: 431 us -> 55.2 us  [per_head(): every = lax.all_gather(mine, ('seq', 'head'), axis=0, tiled=True)]
    reduce_scatter x4 -> x2, waiting for transfers between devices: 427 us -> 146 us  [the longest x1 125 us: per_head(): lax.psum_scatter(partial_input.astype(jnp.bfloat16), 'head', scatter_dime...]
    all_to_all x0 -> x4, waiting for transfers between devices: none -> 198 us  [the longest x1 102 us: per_head(): lax.all_to_all(weights, 'seq', 0, 0, tiled=True).reshape(width, 3 * own)]
    dot_general x21 -> x15, matrix products: 74.4 us -> 52.3 us  [the longest x1 13.7 us: per_head(): jnp.einsum('td,tc->dc', every, gradient, preferred_element_type=jnp.float32)]
    all_to_all x0 -> x4, starting transfers between devices: none -> 20.6 us  [the longest x1 7.25 us: per_head(): lax.all_to_all(weights, 'seq', 0, 0, tiled=True).reshape(width, 3 * own)]
  transfers between devices with their start and end apart: 9 -> 7, of which waited for: 9 -> 6; matrix products, arithmetic and copies ran while one was open for 10% -> 9% of each run, Pallas kernels for 0% -> 0%
where the time goes in v1:
time: 513 us; the launch traced here: 512 us
  waiting for transfers between devices  399 us (78%)
  matrix products  52.3 us (10%)
  local copies, waits for them, and re-layouts  22.4 us (4%)
  starting transfers between devices  20.7 us (4%)
  between operations  14 us (3%)
    reduce_scatter x1, waiting for transfers between devices, per_head(): lax.psum_scatter(partial_input.astype(jnp.bfloat16), 'head', scatter_dime...  125 us
    all_to_all x1, waiting for transfers between devices, per_head(): lax.all_to_all(weights, 'seq', 0, 0, tiled=True).reshape(width, 3 * own)  102 us
    all_to_all x1, waiting for transfers between devices, per_head(): lax.all_to_all(grad_w.astype(jnp.bfloat16).reshape(seq_count, weight_rows...  85.3 us
    all_gather x1, waiting for transfers between devices, per_head(): every = lax.all_gather(mine, ('seq', 'head'), axis=0, tiled=True)  55.2 us
    reduce_scatter x1, waiting for transfers between devices, per_head(): grad_x = lax.psum_scatter(grad_x, 'seq', scatter_dimension=0, tiled=True)  20.8 us
    dot_general x1, matrix products, per_head(): jnp.einsum('td,tc->dc', every, gradient, preferred_element_type=jnp.float32)  13.7 us
    dot_general x1, matrix products, per_head(): jnp.dot(every, weights, preferred_element_type=jnp.float32)  13.3 us
    dot_general x1, matrix products, per_head(): jnp.einsum('tc,dc->td', gradient, weights, preferred_element_type=jnp.flo...  11.8 us
  transfers between devices with their start and end apart: 7, of which 6 were waited for; matrix products, arithmetic and copies ran while one was open for 9% of the time, Pallas kernels for 0%

profile of v1, /device:TPU:0, one launch (start us, length us, event | category | flops | bytes accessed | tf_op | source)
XLA Modules:
  0.0 511.8 jit_solution(3910845758628917875)
XLA Ops:
  7.2 1.5 copy-done
  9.6 1.5 copy.40
  11.7 1.5 copy.42
  13.2 1.8 pad_maximum_fusion
  15.0 7.3 %all-to-all-start = ((bf16[8,512,384]{1,2,0:T(8,128)(2,1)}), bf16[8,512,384]{1,2,0:T(8,128)(2,1)S(1)}, u32[]{:S(2)}, u32[]{:S(2)}) async-start(bf16[8,512,384]{1,2,0:T(8,128)(2,1)} %pad_maximum_fusion), calls=%async_computation | async-start | bytes 6291456 | tf_op jit(solution)/shard_map/all_to_all | solution.py:201
  22.2 2.0 bitcast_bitcast_fusion
  24.2 102.5 %all-to-all-done = bf16[8,512,384]{1,2,0:T(8,128)(2,1)S(1)} async-done(((bf16[8,512,384]{1,2,0:T(8,128)(2,1)}), bf16[8,512,384]{1,2,0:T(8,128)(2,1)S(1)}, u32[]{:S(2)}, u32[]{:S(2)}) %all-to-all-start) | async-done | bytes 3145760 | tf_op jit(solution)/shard_map/all_to_all | solution.py:201
  126.7 4.2 all-to-all-start.2
  130.9 2.8 copy.43
  133.7 55.2 %all-gather.2.cloned.1.call-done = bf16[2048,4096]{1,0:T(8,128)(2,1)} async-done(((bf16[64,4096]{1,0:T(8,128)(2,1)}), bf16[2048,4096]{1,0:T(8,128)(2,1)}) %all-gather.2.cloned.1.call-update) | async-done | bytes 16777232 | tf_op jit(solution)/shard_map/all_gather | solution.py:197
  188.9 13.3 %convolution_convert_fusion.2 = bf16[2048,384]{1,0:T(8,128)(2,1)S(1)} fusion(bf16[2048,4096]{1,0:T(8,128)(2,1)} %all-gather.2.cloned.1.call-done, bf16[4096,384]{1,0:T(8,128)(2,1)} %bitcast.135), kind=kOutput, calls=%fused_computation.3 | convolution fusion | flops 6443237376 | bytes 21495808 | tf_op jit(solution)/shard_map/dot_general | solution.py:204
  202.8 1.5 fusion.9
  204.3 2.4 fusion.29
  207.3 1.5 convolution_multiply_fusion.3
  208.8 1.3 fusion.28
  210.1 1.1 fusion.11
  211.2 2.3 reverse.4
  213.5 1.3 reduce-window_bitcast_fusion
  216.8 1.5 convolution_bitcast_fusion
  218.3 1.7 fusion.6
  221.1 11.8 %convolution_convert_fusion = bf16[2048,4096]{1,0:T(8,128)(2,1)} fusion(bf16[4096,384]{1,0:T(8,128)(2,1)S(1)} %bitcast.136, bf16[2048,128]{1,0:T(8,128)(2,1)S(1)} %bitcast.143, bf16[2048,128]{1,0:T(8,128)(2,1)S(1)} %bitcast.141, bf16[2048,128]{1,0:T(8,128)(2,1)S(1)} %bitcast.139), kind=kOutput, calls=%fused_computation | convolution fusion | flops 6455558144 | bytes 21495808 | tf_op jit(solution)/shard_map/tc,dc->td/dot_general | solution.py:212
  233.0 125.2 %reduce-scatter.3.cloned.1.call-done = bf16[2048,1024]{1,0:T(8,128)(2,1)} async-done(((bf16[2048,4096]{1,0:T(8,128)(2,1)}), bf16[2048,1024]{1,0:T(8,128)(2,1)}) %reduce-scatter.3.cloned.1.call-update) | async-done | bytes 4194320 | tf_op jit(solution)/shard_map/reduce_scatter | solution.py:213
  358.5 1.1 fusion.7
  359.6 5.5 %all-to-all-start.1 = ((bf16[8,256,128]{2,1,0:T(8,128)(2,1)}), bf16[8,256,128]{2,1,0:T(8,128)(2,1)S(1)}, u32[]{:S(2)}, u32[]{:S(2)}) async-start(bf16[8,256,128]{2,1,0:T(8,128)(2,1)} %bitcast.16), calls=%async_computation.1 | async-start | bytes 1048576 | tf_op jit(solution)/shard_map/all_to_all | solution.py:209
  365.1 13.7 %convolution_convert_fusion.1 = bf16[4096,384]{1,0:T(8,128)(2,1)} fusion(bf16[2048,4096]{1,0:T(8,128)(2,1)} %all-gather.2.cloned.1.call-done, bf16[2048,128]{1,0:T(8,128)(2,1)} %bitcast.144, bf16[2048,128]{1,0:T(8,128)(2,1)S(1)} %bitcast.142, bf16[2048,128]{1,0:T(8,128)(2,1)S(1)} %bitcast.140), kind=kOutput, calls=%fused_computation.1 | convolution fusion | flops 6448742400 | bytes 21495808 | tf_op jit(solution)/shard_map/td,tc->dc/dot_general | solution.py:217
  378.8 10.2 %all-to-all-done.1 = bf16[8,256,128]{2,1,0:T(8,128)(2,1)S(1)} async-done(((bf16[8,256,128]{2,1,0:T(8,128)(2,1)}), bf16[8,256,128]{2,1,0:T(8,128)(2,1)S(1)}, u32[]{:S(2)}, u32[]{:S(2)}) %all-to-all-start.1) | async-done | bytes 524320 | tf_op jit(solution)/shard_map/all_to_all | solution.py:209
  389.9 3.7 all-to-all-start.3
  393.5 1.9 copy_bitcast_fusion.3
  395.4 85.3 %all-to-all-done.3 = bf16[8,512,384]{2,1,0:T(8,128)(2,1)S(1)} async-done(((bf16[8,512,384]{2,1,0:T(8,128)(2,1)}), bf16[8,512,384]{2,1,0:T(8,128)(2,1)S(1)}, u32[]{:S(2)}, u32[]{:S(2)}) %all-to-all-start.3) | async-done | bytes 3145760 | tf_op jit(solution)/shard_map/all_to_all | solution.py:218
  481.6 1.3 copy.74
  482.9 1.6 copy_bitcast_fusion
  484.5 20.8 %reduce-scatter.5.cloned.1.call-done = bf16[256,1024]{1,0:T(8,128)(2,1)} async-done(((bf16[2048,1024]{1,0:T(8,128)(2,1)}), bf16[256,1024]{1,0:T(8,128)(2,1)}) %reduce-scatter.5.cloned.1.call-update) | async-done | bytes 524304 | tf_op jit(solution)/shard_map/reduce_scatter | solution.py:216
  (39 shorter events, 7.7 us)
Async XLA Ops:
  7.2 1.6 copy-start
  7.2 3.9 copy-start.4
  7.2 181.7 %all-gather.2.cloned.1.call-start = ((), (), s32[]{:S(2)}) async-start(), calls=%async_computation.6 | async-start | bytes 17301504 | tf_op jit(solution)/shard_map/all_gather | solution.py:197
  15.0 111.7 %all-to-all-start = ((bf16[8,512,384]{1,2,0:T(8,128)(2,1)}), bf16[8,512,384]{1,2,0:T(8,128)(2,1)S(1)}, u32[]{:S(2)}, u32[]{:S(2)}) async-start(bf16[8,512,384]{1,2,0:T(8,128)(2,1)} %pad_maximum_fusion), calls=%async_computation | async-start | bytes 6291456 | tf_op jit(solution)/shard_map/all_to_all | solution.py:201
  126.7 76.1 %all-to-all-start.2 = ((bf16[8,256,128]{2,1,0:T(8,128)(2,1)}), bf16[8,256,128]{2,1,0:T(8,128)(2,1)}, u32[]{:S(2)}, u32[]{:S(2)}) async-start(bf16[8,256,128]{2,1,0:T(8,128)(2,1)} %bitcast_bitcast_fusion), calls=%async_computation.2 | async-start | bytes 1048576 | tf_op jit(solution)/shard_map/all_to_all | solution.py:202
  130.8 227.3 %reduce-scatter.3.cloned.1.call-start = ((), (), s32[]{:S(2)}) async-start(), calls=%async_computation.7 | async-start | bytes 20971520 | tf_op jit(solution)/shard_map/reduce_scatter | solution.py:213
  216.7 4.4 copy-start.2
  216.7 4.4 copy-start.5
  220.0 0.8 copy-start.7
  220.3 0.8 copy-start.9
  232.9 272.4 %reduce-scatter.5.cloned.1.call-start = ((), (), s32[]{:S(2)}) async-start(), calls=%async_computation.8 | async-start | bytes 4718592 | tf_op jit(solution)/shard_map/reduce_scatter | solution.py:216
  358.5 6.6 %copy-start.6 = (bf16[16,128,128]{1,2,0:T(8,128)(2,1)S(1)}, bf16[16,128,128]{1,2,0:T(8,128)(2,1)}, u32[]{:S(2)}) copy-start(bf16[16,128,128]{1,2,0:T(8,128)(2,1)} %fusion.11) | copy-start | bytes 1572868
  358.5 6.6 %copy-start.8 = (bf16[16,128,128]{1,2,0:T(8,128)(2,1)S(1)}, bf16[16,128,128]{1,2,0:T(8,128)(2,1)}, u32[]{:S(2)}) copy-start(bf16[16,128,128]{1,2,0:T(8,128)(2,1)} %copy-done.7) | copy-start | bytes 1572868
  359.6 29.5 %all-to-all-start.1 = ((bf16[8,256,128]{2,1,0:T(8,128)(2,1)}), bf16[8,256,128]{2,1,0:T(8,128)(2,1)S(1)}, u32[]{:S(2)}, u32[]{:S(2)}) async-start(bf16[8,256,128]{2,1,0:T(8,128)(2,1)} %bitcast.16), calls=%async_computation.1 | async-start | bytes 1048576 | tf_op jit(solution)/shard_map/all_to_all | solution.py:209
  389.1 0.8 copy-start.3
  389.9 90.9 %all-to-all-start.3 = ((bf16[8,512,384]{2,1,0:T(8,128)(2,1)}), bf16[8,512,384]{2,1,0:T(8,128)(2,1)S(1)}, u32[]{:S(2)}, u32[]{:S(2)}) async-start(bf16[8,512,384]{2,1,0:T(8,128)(2,1)} %bitcast.137), calls=%async_computation.5 | async-start | bytes 6291456 | tf_op jit(solution)/shard_map/all_to_all | solution.py:218
  481.6 23.7 %copy-start.1 = (bf16[256,4096]{1,0:T(8,128)(2,1)S(1)}, bf16[256,4096]{1,0:T(8,128)(2,1)}, u32[]{:S(2)}) copy-start(bf16[256,4096]{1,0:T(8,128)(2,1)} %param.5) | copy-start | bytes 6291460
Sparse Core Ops, SparseCore 0:
  11.5 177.3 all-gather.1
  233.0 125.0 reduce-scatter.2
  362.8 142.4 reduce-scatter.4

commit v2 on v1

--- a/solution.py
+++ b/solution.py
@@ -186,22 +186,79 @@
     return jnp.transpose(pieces, (1, 0, 2)).reshape(pieces.shape[1], -1)
 
 
+BOTH = ("seq", "head")
+Z1, Z0, X, Y, CORE = 16, 8, 4, 2, 1
+
+
+def swap(value, bit):
+    count = lax.axis_size("seq") * lax.axis_size("head")
+    return lax.ppermute(value, BOTH, [(i, i ^ bit) for i in range(count)])
+
+
+def gather_rows(piece, bits):
+    for bit in bits[:-1]:
+        piece = jnp.concatenate([piece, swap(piece, bit)], axis=0)
+    return [piece, swap(piece, bits[-1])]
+
+
+def block_places(me, bits):
+    index = jnp.arange(1 << len(bits), dtype=jnp.int32)
+    place = jnp.zeros_like(index)
+    for k, bit in enumerate(bits):
+        place = place + ((index >> k) & 1) * bit
+    return place ^ me
+
+
+def joined(mine, theirs):
+    return (mine.astype(jnp.float32) + theirs.astype(jnp.float32)).astype(jnp.bfloat16)
+
+
+def fold(value, bit):
+    half = value.shape[0] // 2
+    return joined(value[:half], swap(value[half:], bit))
+
+
+def select_rows(source_row, wanted_row, matrix):
+    chosen = (wanted_row[:, None] == source_row[None, :]).astype(jnp.bfloat16)
+    return jnp.dot(chosen, matrix, preferred_element_type=jnp.float32).astype(jnp.bfloat16)
+
+
 def per_head(tokens, w_query, w_key, w_value, grad_out):
     seq_count, head_axis = lax.axis_size("seq"), lax.axis_size("head")
     tok_rows, width = tokens.shape
     weight_rows, col_count = w_query.shape
     own = col_count // seq_count
-    score_scale = 1.0 / math.sqrt(HD * tok_rows * seq_count)
+    tok_count = tok_rows * seq_count
+    score_scale = 1.0 / math.sqrt(HD * tok_count)
     share = tok_rows // head_axis
-    mine = lax.dynamic_slice_in_dim(tokens, lax.axis_index("head") * share, share, 0)
-    every = lax.all_gather(mine, ("seq", "head"), axis=0, tiled=True)
+    seat = lax.axis_index("head")
+    me = lax.axis_index("seq") * head_axis + seat
+    mine = lax.dynamic_slice_in_dim(tokens, seat * share, share, 0)
+
+    orders = ((Z1, Z0, X, Y, CORE), (Z1, Z0, Y, X, CORE))
+    part = share // 2
+    pieces, gathered_row = [], []
+    for k, bits in enumerate(orders):
+        pieces += gather_rows(mine[k * part : (k + 1) * part], bits)
+        starts = block_places(me, bits) * share + k * part
+        gathered_row.append((starts[:, None] + jnp.arange(part)[None, :]).reshape(-1))
+    gathered_row = jnp.concatenate(gathered_row)
+
     weights = jnp.concatenate(
         [columns_first(w, seq_count) for w in (w_query, w_key, w_value)], axis=2
     )
     weights = lax.all_to_all(weights, "seq", 0, 0, tiled=True).reshape(width, 3 * own)
     grads = lax.all_to_all(columns_first(grad_out, seq_count), "seq", 0, 0, tiled=True)
-    grads = grads.reshape(tok_rows * seq_count, own)
-    projected = jnp.dot(every, weights, preferred_element_type=jnp.float32).astype(jnp.bfloat16)
+    grads = grads.reshape(tok_count, own)
+    projected = jnp.concatenate(
+        [
+            jnp.dot(p, weights, preferred_element_type=jnp.float32).astype(jnp.bfloat16)
+            for p in pieces
+        ],
+        axis=0,
+    )
+    rows = jnp.arange(tok_count, dtype=jnp.int32)
+    projected = select_rows(gathered_row, rows, projected)
     attn_out, grad_q, grad_k, grad_v = head_attention(
         projected[:, :own], projected[:, own : 2 * own], projected[:, 2 * own :], grads, score_scale
     )
@@ -209,12 +266,41 @@
         lax.all_to_all(attn_out.reshape(seq_count, tok_rows, own), "seq", 0, 0, tiled=True)
     )
     gradient = jnp.concatenate([grad_q, grad_k, grad_v], axis=1)
-    partial_input = jnp.einsum("tc,dc->td", gradient, weights, preferred_element_type=jnp.float32)
-    grad_x = lax.psum_scatter(
-        partial_input.astype(jnp.bfloat16), "head", scatter_dimension=1, tiled=True
-    )
-    grad_x = lax.psum_scatter(grad_x, "seq", scatter_dimension=0, tiled=True)
-    grad_w = jnp.einsum("td,tc->dc", every, gradient, preferred_element_type=jnp.float32)
+
+    half_rows = tok_rows // 2
+    seq_starts = (block_places(me, (Z1, Z0, X)) // head_axis) * tok_rows
+    half_starts = jnp.concatenate([seq_starts, seq_starts + half_rows])
+    scattered_row = (half_starts[:, None] + jnp.arange(half_rows)[None, :]).reshape(-1)
+    placed = select_rows(rows, scattered_row, gradient)
+
+    def term(other):
+        chosen = lax.dynamic_slice_in_dim(
+            weights, (seat ^ other) * (width // head_axis), width // head_axis, 0
+        )
+        return jnp.einsum("tc,dc->td", placed, chosen, preferred_element_type=jnp.float32).astype(
+            jnp.bfloat16
+        )
+
+    far = swap(term(Y | CORE), CORE)
+    near = swap(term(CORE), CORE)
+    far = joined(term(Y), far)
+    near = joined(term(0), near)
+    middle = tok_count // 2
+    quarter = middle // 2
+    first = joined(near[:middle], swap(far[:middle], Y))
+    first = fold(first, X)
+    second_far = joined(far[middle : middle + quarter], swap(far[middle + quarter :], X))
+    second_near = joined(near[middle : middle + quarter], swap(near[middle + quarter :], X))
+    second = joined(second_near, swap(second_far, Y))
+    grad_x = jnp.concatenate([fold(fold(v, Z0), Z1) for v in (first, second)], axis=0)
+
+    matching = select_rows(rows, gathered_row, gradient)
+    grad_w, lower = 0.0, 0
+    for p in pieces:
+        grad_w = grad_w + jnp.einsum(
+            "td,tc->dc", p, matching[lower : lower + p.shape[0]], preferred_element_type=jnp.float32
+        )
+        lower += p.shape[0]
     grad_w = lax.all_to_all(
         grad_w.astype(jnp.bfloat16).reshape(seq_count, weight_rows, 3 * own), "seq", 0, 0, tiled=True
     )
@@ -243,7 +329,7 @@
     def whole(tokens, w_query, w_key, w_value, grad_out):
         seq_count, head_axis = mesh.shape["seq"], mesh.shape["head"]
         heads = w_query.shape[1] // HD
-        even = heads % (seq_count * head_axis) == 0 and tokens.shape[0] % (seq_count * head_axis) == 0
+        even = (seq_count, head_axis) == (8, 4) and heads % (seq_count * head_axis) == 0
         return mapped(per_head if even else per_device)(tokens, w_query, w_key, w_value, grad_out)
 
     def mapped(body):

time: 513 us -> 395 us (0.77)
  waiting for transfers between devices: 399 us -> 205 us
  matrix products: 52.3 us -> 85 us
  starting transfers between devices: 20.7 us -> 47.2 us
  local copies, waits for them, and re-layouts: 22.4 us -> 37.7 us
  between operations: 14 us -> 1.79 us
  other arithmetic: 3.18 us -> 13.5 us
    ppermute x0 -> x21, waiting for transfers between devices: none -> 205 us  [swap(): return lax.ppermute(value, BOTH, [(i, i ^ bit) for i in range(count)])]
    reduce_scatter x2 -> x0, waiting for transfers between devices: 146 us -> none  [the longest x1 125 us: per_head(): lax.psum_scatter(partial_input.astype(jnp.bfloat16), 'head', scatter_dime...]
    all_to_all x1, waiting for transfers between devices: 102 us -> 0.01 us  [per_head(): lax.all_to_all(weights, 'seq', 0, 0, tiled=True).reshape(width, 3 * own)]
    all_to_all x1, waiting for transfers between devices: 85.3 us -> 0.01 us  [per_head(): lax.all_to_all(grad_w.astype(jnp.bfloat16).reshape(seq_count, weight_rows...]
    all_gather x1 -> x0, waiting for transfers between devices: 55.2 us -> none  [per_head(): every = lax.all_gather(mine, ('seq', 'head'), axis=0, tiled=True)]
    dot_general x3 -> x15, matrix products: 38.7 us -> 73.5 us  [the longest x4 21 us: per_head(): jnp.einsum('td,tc->dc', p, matching[lower:lower + p.shape[0]], preferred_...]
    ppermute x0 -> x21, starting transfers between devices: none -> 24.7 us  [swap(): return lax.ppermute(value, BOTH, [(i, i ^ bit) for i in range(count)])]
    all_to_all x1, waiting for transfers between devices: 10.2 us -> 0.01 us  [per_head(): lax.all_to_all(attn_out.reshape(seq_count, tok_rows, own), 'seq', 0, 0, t...]
  transfers between devices with their start and end apart: 7 -> 25, of which waited for: 6 -> 12; matrix products, arithmetic and copies ran while one was open for 9% -> 32% of each run, Pallas kernels for 0% -> 0%
where the time goes in v2:
time: 395 us; the launch traced here: 390 us
  waiting for transfers between devices  205 us (52%)
  matrix products  85 us (22%)
  starting transfers between devices  47.2 us (12%)
  local copies, waits for them, and re-layouts  37.7 us (10%)
  other arithmetic  13.5 us (3%)
    ppermute x21, waiting for transfers between devices, swap(): return lax.ppermute(value, BOTH, [(i, i ^ bit) for i in range(count)])  205 us
    ppermute x21, starting transfers between devices, swap(): return lax.ppermute(value, BOTH, [(i, i ^ bit) for i in range(count)])  24.7 us
    dot_general x4, matrix products, per_head(): jnp.einsum('td,tc->dc', p, matching[lower:lower + p.shape[0]], preferred_...  21 us
    dot_general x4, matrix products, term(): jnp.einsum('tc,dc->td', placed, chosen, preferred_element_type=jnp.float32)  19.2 us
    dot_general x4, matrix products, per_head(): jnp.dot(p, weights, preferred_element_type=jnp.float32).astype(jnp.bfloat16)  19.2 us
    unnamed x48, local copies, waits for them, and re-layouts  15.1 us
    dot_general x3, matrix products, select_rows(): jnp.dot(chosen, matrix, preferred_element_type=jnp.float32)  14 us
  transfers between devices with their start and end apart: 25, of which 12 were waited for; matrix products, arithmetic and copies ran while one was open for 32% of the time, Pallas kernels for 0%

profile of v2, /device:TPU:0, one launch (start us, length us, event | category | flops | bytes accessed | tf_op | source)
XLA Modules:
  0.0 390.1 jit_solution(11700414896416501701)
XLA Ops:
  2.7 4.0 %collective-permute-start = (bf16[32,4096]{1,0:T(8,128)(2,1)S(1)}, bf16[32,4096]{1,0:T(8,128)(2,1)S(1)}, u32[]{:S(2)}, u32[]{:S(2)}) collective-permute-start(bf16[32,4096]{1,0:T(8,128)(2,1)S(1)} %get-tuple-element.6), channel_id=1, source_target_pairs={{0,16},{1,17},{2,18},{3,19},{4,20},{5,21},{6,22},{7,23},{8,24},{9,... | collective-permute-start | bytes 786440 | tf_op jit(solution)/shard_map/ppermute | solution.py:195
  6.7 18.3 %collective-permute-done = bf16[32,4096]{1,0:T(8,128)(2,1)S(1)} collective-permute-done((bf16[32,4096]{1,0:T(8,128)(2,1)S(1)}, bf16[32,4096]{1,0:T(8,128)(2,1)S(1)}, u32[]{:S(2)}, u32[]{:S(2)}) %collective-permute-start) | collective-permute-done | bytes 262176 | tf_op jit(solution)/shard_map/ppermute | solution.py:195
  34.9 6.3 %collective-permute-done.1 = bf16[64,4096]{1,0:T(8,128)(2,1)S(1)} collective-permute-done((bf16[64,4096]{1,0:T(8,128)(2,1)S(1)}, bf16[64,4096]{1,0:T(8,128)(2,1)S(1)}, u32[]{:S(2)}, u32[]{:S(2)}) %collective-permute-start.1) | collective-permute-done | bytes 524320 | tf_op jit(solution)/shard_map/ppermute | solution.py:195
  45.6 4.8 %all-to-all-start = ((bf16[8,512,384]{1,2,0:T(8,128)(2,1)}), bf16[8,512,384]{1,2,0:T(8,128)(2,1)}, u32[]{:S(2)}, u32[]{:S(2)}) async-start(bf16[8,512,384]{1,2,0:T(8,128)(2,1)} %pad_maximum_fusion), calls=%async_computation | async-start | bytes 6291456 | tf_op jit(solution)/shard_map/all_to_all | solution.py:250
  54.8 31.1 %collective-permute-done.2 = bf16[128,4096]{1,0:T(8,128)(2,1)S(1)} collective-permute-done((bf16[128,4096]{1,0:T(8,128)(2,1)}, bf16[128,4096]{1,0:T(8,128)(2,1)S(1)}, u32[]{:S(2)}, u32[]{:S(2)}) %collective-permute-start.2) | collective-permute-done | bytes 1048608 | tf_op jit(solution)/shard_map/ppermute | solution.py:195
  94.7 37.9 %collective-permute-done.3 = bf16[256,4096]{1,0:T(8,128)(2,1)S(1)} collective-permute-done((bf16[256,4096]{1,0:T(8,128)(2,1)S(1)}, bf16[256,4096]{1,0:T(8,128)(2,1)S(1)}, u32[]{:S(2)}, u32[]{:S(2)}) %collective-permute-start.3) | collective-permute-done | bytes 2097184 | tf_op jit(solution)/shard_map/ppermute | solution.py:195
  135.2 10.9 %collective-permute-done.8 = bf16[256,4096]{1,0:T(8,128)(2,1)S(1)} collective-permute-done((bf16[256,4096]{1,0:T(8,128)(2,1)S(1)}, bf16[256,4096]{1,0:T(8,128)(2,1)S(1)}, u32[]{:S(2)}, u32[]{:S(2)}) %collective-permute-start.8) | collective-permute-done | bytes 2097184 | tf_op jit(solution)/shard_map/ppermute | solution.py:195
  149.1 5.7 %all-to-all-start.2 = ((bf16[8,256,128]{2,1,0:T(8,128)(2,1)}), bf16[8,256,128]{2,1,0:T(8,128)(2,1)S(1)}, u32[]{:S(2)}, u32[]{:S(2)}) async-start(bf16[8,256,128]{2,1,0:T(8,128)(2,1)} %bitcast_bitcast_fusion), calls=%async_computation.2 | async-start | bytes 1048576 | tf_op jit(solution)/shard_map/all_to_all | solution.py:251
  154.8 4.8 %copy.43 = bf16[8,512,384]{2,1,0:T(8,128)(2,1)} copy(bf16[8,512,384]{1,2,0:T(8,128)(2,1)} %all-to-all-done) | data formatting | bytes 6291456 | tf_op jit(solution)/shard_map/all_to_all | solution.py:250
  159.7 5.6 %convolution_convert_fusion.3 = bf16[512,384]{1,0:T(8,128)(2,1)S(1)} fusion(bf16[512,4096]{1,0:T(8,128)(2,1)} %constant_dynamic-update-slice_fusion.6, bf16[4096,384]{1,0:T(8,128)(2,1)} %bitcast.155), kind=kOutput, calls=%fused_computation.55 | convolution fusion | flops 1610809344 | bytes 7733248 | tf_op jit(solution)/shard_map/dot_general | solution.py:255
  165.3 4.5 %convolution_convert_fusion.5 = bf16[512,384]{1,0:T(8,128)(2,1)S(1)} fusion(bf16[512,4096]{1,0:T(8,128)(2,1)} %constant_dynamic-update-slice_fusion.1, bf16[4096,384]{1,0:T(8,128)(2,1)S(1)} %bitcast.158), kind=kOutput, calls=%fused_computation.57 | convolution fusion | flops 1610809344 | bytes 7733248 | tf_op jit(solution)/shard_map/dot_general | solution.py:255
  169.9 4.5 %convolution_convert_fusion.4 = bf16[512,384]{1,0:T(8,128)(2,1)S(1)} fusion(bf16[512,4096]{1,0:T(8,128)(2,1)} %collective-permute-done.4, bf16[4096,384]{1,0:T(8,128)(2,1)S(1)} %bitcast.159), kind=kOutput, calls=%fused_computation.56 | convolution fusion | flops 1610809344 | bytes 7733248 | tf_op jit(solution)/shard_map/dot_general | solution.py:255
  174.4 4.5 %convolution_convert_fusion.2 = bf16[512,384]{1,0:T(8,128)(2,1)S(1)} fusion(bf16[512,4096]{1,0:T(8,128)(2,1)} %collective-permute-done.9, bf16[4096,384]{1,0:T(8,128)(2,1)S(1)} %bitcast.160), kind=kOutput, calls=%fused_computation.54 | convolution fusion | flops 1610809344 | bytes 7733248 | tf_op jit(solution)/shard_map/dot_general | solution.py:255
  179.0 4.5 %fusion.8 = bf16[2048,384]{1,0:T(8,128)(2,1)S(1)} fusion(s32[2048]{0:T(1024)S(1)} %constant_dynamic-update-slice_fusion.11, bf16[512,384]{1,0:T(8,128)(2,1)S(1)} %convolution_convert_fusion.2, bf16[512,384]{1,0:T(8,128)(2,1)S(1)} %convolution_convert_fusion.3, bf16[512,384]{1,0:T(8,128)(2,1)S(1)} %convolution_convert_fusion.4, ...), kind=kOutput, calls=%fused_computation.18 | convolution fusion | flops 3232497664 | bytes 3153920 | tf_op jit(solution)/shard_map/dot_general | solution.py:223
  193.5 6.0 %all-to-all-start.1 = ((bf16[8,256,128]{2,1,0:T(8,128)(2,1)}), bf16[8,256,128]{2,1,0:T(8,128)(2,1)}, u32[]{:S(2)}, u32[]{:S(2)}) async-start(bf16[8,256,128]{2,1,0:T(8,128)(2,1)} %bitcast.16), calls=%async_computation.1 | async-start | bytes 1048576 | tf_op jit(solution)/shard_map/all_to_all | solution.py:266
  205.3 4.7 %fusion.7 = bf16[2048,384]{1,0:T(8,128)(2,1)S(1)} fusion(s32[2048]{0:T(1024)S(1)} %add_bitcast_fusion, bf16[2048,128]{1,0:T(8,128)(2,1)S(1)} %bitcast.168, bf16[2048,128]{1,0:T(8,128)(2,1)S(1)} %bitcast.166, bf16[2048,128]{1,0:T(8,128)(2,1)S(1)} %bitcast.170), kind=kOutput, calls=%fused_computation.17 | convolution fusion | flops 3230924800 | bytes 3153920 | tf_op jit(solution)/shard_map/dot_general | solution.py:223
  210.0 4.3 %convolution_convert_fusion = bf16[2048,1024]{1,0:T(8,128)(2,1)} fusion(bf16[2048,384]{1,0:T(8,128)(2,1)S(1)} %fusion.7, bf16[4096,384]{1,0:T(8,128)(2,1)S(1)} %bitcast.161, s32[]{:T(128)S(6)} %select_n.36), kind=kOutput, calls=%fused_computation.13 | convolution fusion | flops 1612709888 | bytes 6553604 | tf_op jit(solution)/shard_map/tc,dc->td/dot_general | solution.py:280
  214.3 4.3 %convolution_convert_fusion.1 = bf16[2048,1024]{1,0:T(8,128)(2,1)} fusion(bf16[2048,384]{1,0:T(8,128)(2,1)S(1)} %fusion.7, bf16[4096,384]{1,0:T(8,128)(2,1)S(1)} %bitcast.162, s32[]{:T(128)S(6)} %select_n.34), kind=kOutput, calls=%fused_computation.14 | convolution fusion | flops 1612709888 | bytes 6553604 | tf_op jit(solution)/shard_map/tc,dc->td/dot_general | solution.py:280
  219.1 4.9 %fusion.6 = bf16[2048,384]{1,0:T(8,128)(2,1)S(1)} fusion(s32[2048]{0:T(1024)S(1)} %constant_dynamic-update-slice_fusion.11, bf16[2048,128]{1,0:T(8,128)(2,1)S(1)} %bitcast.169, bf16[2048,128]{1,0:T(8,128)(2,1)S(1)} %bitcast.167, bf16[2048,128]{1,0:T(8,128)(2,1)S(1)} %bitcast.171), kind=kOutput, calls=%fused_computation.16 | convolution fusion | flops 3230924800 | bytes 3153920 | tf_op jit(solution)/shard_map/dot_general | solution.py:223
  224.0 4.6 %fusion.45 = f32[4096,384]{1,0:T(8,128)S(1)} fusion(bf16[512,4096]{1,0:T(8,128)(2,1)} %constant_dynamic-update-slice_fusion.6, bf16[2048,384]{1,0:T(8,128)(2,1)S(1)} %fusion.6), kind=kOutput, calls=%fused_computation.94 | convolution fusion | flops 1610612736 | bytes 10878976 | tf_op jit(solution)/shard_map/td,tc->dc/dot_general | solution.py:300
  228.6 4.6 %fusion.49 = f32[4096,384]{1,0:T(8,128)S(1)} fusion(bf16[512,4096]{1,0:T(8,128)(2,1)} %constant_dynamic-update-slice_fusion.1, bf16[2048,384]{1,0:T(8,128)(2,1)S(1)} %fusion.6), kind=kOutput, calls=%fused_computation.98 | convolution fusion | flops 1610612736 | bytes 10878976 | tf_op jit(solution)/shard_map/td,tc->dc/dot_general | solution.py:300
  233.2 4.6 %fusion.47 = f32[4096,384]{1,0:T(8,128)S(1)} fusion(bf16[512,4096]{1,0:T(8,128)(2,1)} %collective-permute-done.4, bf16[2048,384]{1,0:T(8,128)(2,1)S(1)} %fusion.6), kind=kOutput, calls=%fused_computation.96 | convolution fusion | flops 1610612736 | bytes 10878976 | tf_op jit(solution)/shard_map/td,tc->dc/dot_general | solution.py:300
  237.9 7.1 %add_convert_fusion.2 = bf16[4096,384]{1,0:T(8,128)(2,1)} fusion(f32[4096,384]{1,0:T(8,128)S(1)} %fusion.45, f32[4096,384]{1,0:T(8,128)S(1)} %fusion.49, f32[4096,384]{1,0:T(8,128)S(1)} %fusion.47, bf16[512,4096]{1,0:T(8,128)(2,1)} %collective-permute-done.9, bf16[2048,384]{1,0:T(8,128)(2,1)S(1)} %fusion.6), kind=kOutput, calls=%fused_computation.11 | convolution fusion | flops 1616904192 | bytes 26607616 | tf_op jit(solution)/shard_map/td,tc->dc/dot_general | solution.py:300
  245.0 6.0 %all-to-all-start.3 = ((bf16[8,512,384]{2,1,0:T(8,128)(2,1)}), bf16[8,512,384]{2,1,0:T(8,128)(2,1)S(1)}, u32[]{:S(2)}, u32[]{:S(2)}) async-start(bf16[8,512,384]{2,1,0:T(8,128)(2,1)} %bitcast.36), calls=%async_computation.3 | async-start | bytes 6291456 | tf_op jit(solution)/shard_map/all_to_all | solution.py:304
  251.0 5.3 %add_convert_fusion = bf16[2048,1024]{1,0:T(8,128)(2,1)S(1)} fusion(bf16[2048,1024]{1,0:T(8,128)(2,1)} %collective-permute-done.11, bf16[2048,384]{1,0:T(8,128)(2,1)} %copy-done.17, bf16[4096,384]{1,0:T(8,128)(2,1)} %bitcast.156, s32[]{:T(128)S(6)} %select_n.35), kind=kOutput, calls=%fused_computation.7 | convolution fusion | flops 1621098496 | bytes 10747908 | tf_op jit(solution)/shard_map/tc,dc->td/dot_general | solution.py:280
  262.5 5.3 %add_convert_fusion.1 = bf16[2048,1024]{1,0:T(8,128)(2,1)S(1)} fusion(bf16[2048,1024]{1,0:T(8,128)(2,1)} %collective-permute-done.10, bf16[2048,384]{1,0:T(8,128)(2,1)} %copy-done.17, bf16[4096,384]{1,0:T(8,128)(2,1)} %bitcast.157, s32[]{:T(128)S(6)} %select_n.33), kind=kOutput, calls=%fused_computation.8 | convolution fusion | flops 1621098496 | bytes 10747908 | tf_op jit(solution)/shard_map/tc,dc->td/dot_general | solution.py:280
  268.0 42.3 %collective-permute-done.17 = bf16[512,1024]{1,0:T(8,128)(2,1)} collective-permute-done((bf16[512,1024]{1,0:T(8,128)(2,1)}, bf16[512,1024]{1,0:T(8,128)(2,1)}, u32[]{:S(2)}, u32[]{:S(2)}) %collective-permute-start.17) | collective-permute-done | bytes 1048608 | tf_op jit(solution)/shard_map/ppermute | solution.py:195
  317.1 15.6 %collective-permute-done.16 = bf16[512,1024]{1,0:T(8,128)(2,1)S(1)} collective-permute-done((bf16[512,1024]{1,0:T(8,128)(2,1)S(1)}, bf16[512,1024]{1,0:T(8,128)(2,1)S(1)}, u32[]{:S(2)}, u32[]{:S(2)}) %collective-permute-start.16) | collective-permute-done | bytes 1048608 | tf_op jit(solution)/shard_map/ppermute | solution.py:195
  332.6 3.8 collective-permute-done.18
  337.2 17.4 %collective-permute-done.13 = bf16[512,1024]{1,0:T(8,128)(2,1)S(1)} collective-permute-done((bf16[512,1024]{1,0:T(8,128)(2,1)S(1)}, bf16[512,1024]{1,0:T(8,128)(2,1)S(1)}, u32[]{:S(2)}, u32[]{:S(2)}) %collective-permute-start.13) | collective-permute-done | bytes 1048608 | tf_op jit(solution)/shard_map/ppermute | solution.py:195
  362.3 11.8 %collective-permute-done.14 = bf16[256,1024]{1,0:T(8,128)(2,1)S(1)} collective-permute-done((bf16[256,1024]{1,0:T(8,128)(2,1)S(1)}, bf16[256,1024]{1,0:T(8,128)(2,1)S(1)}, u32[]{:S(2)}, u32[]{:S(2)}) %collective-permute-start.14) | collective-permute-done | bytes 524320 | tf_op jit(solution)/shard_map/ppermute | solution.py:195
  380.6 7.4 %collective-permute-done.15 = bf16[128,1024]{1,0:T(8,128)(2,1)} collective-permute-done((bf16[128,1024]{1,0:T(8,128)(2,1)}, bf16[128,1024]{1,0:T(8,128)(2,1)}, u32[]{:S(2)}, u32[]{:S(2)}) %collective-permute-start.15) | collective-permute-done | bytes 262176 | tf_op jit(solution)/shard_map/ppermute | solution.py:195
  (142 shorter events, 80.5 us)
Async XLA Ops:
  0.6 147.6 %copy-start = (bf16[256,1024]{1,0:T(8,128)(2,1)S(1)}, bf16[256,1024]{1,0:T(8,128)(2,1)}, u32[]{:S(2)}) copy-start(bf16[256,1024]{1,0:T(8,128)(2,1)} %param.9) | copy-start | bytes 1572868
  2.7 38.5 %copy-start.7 = (bf16[32,4096]{1,0:T(8,128)(2,1)}, bf16[32,4096]{1,0:T(8,128)(2,1)S(1)}, u32[]{:S(2)}) copy-start(bf16[32,4096]{1,0:T(8,128)(2,1)S(1)} %get-tuple-element.6) | copy-start | bytes 786436
  2.7 22.4 %collective-permute-start = (bf16[32,4096]{1,0:T(8,128)(2,1)S(1)}, bf16[32,4096]{1,0:T(8,128)(2,1)S(1)}, u32[]{:S(2)}, u32[]{:S(2)}) collective-permute-start(bf16[32,4096]{1,0:T(8,128)(2,1)S(1)} %get-tuple-element.6), channel_id=1, source_target_pairs={{0,16},{1,17},{2,18},{3,19},{4,20},{5,21},{6,22},{7,23},{8,24},{9,... | collective-permute-start | bytes 786440 | tf_op jit(solution)/shard_map/ppermute | solution.py:195
  6.7 25.3 %collective-permute-start.5 = (bf16[32,4096]{1,0:T(8,128)(2,1)S(1)}, bf16[32,4096]{1,0:T(8,128)(2,1)S(1)}, u32[]{:S(2)}, u32[]{:S(2)}) collective-permute-start(bf16[32,4096]{1,0:T(8,128)(2,1)S(1)} %get-tuple-element.13), channel_id=1, source_target_pairs={{0,16},{1,17},{2,18},{3,19},{4,20},{5,21},{6,22},{7,23},{8,24},{9,... | collective-permute-start | bytes 786440 | tf_op jit(solution)/shard_map/ppermute | solution.py:195
  25.1 16.1 %collective-permute-start.1 = (bf16[64,4096]{1,0:T(8,128)(2,1)S(1)}, bf16[64,4096]{1,0:T(8,128)(2,1)S(1)}, u32[]{:S(2)}, u32[]{:S(2)}) collective-permute-start(bf16[64,4096]{1,0:T(8,128)(2,1)S(1)} %pad_maximum_fusion.8), channel_id=1, source_target_pairs={{0,8},{1,9},{2,10},{3,11},{4,12},{5,13},{6,14},{7,15},{8,0},{9,1},... | collective-permute-start | bytes 1572872 | tf_op jit(solution)/shard_map/ppermute | solution.py:195
  32.0 11.8 %copy-start.4 = (bf16[512,1024]{0,1:T(8,128)(2,1)S(1)}, bf16[512,1024]{0,1:T(8,128)(2,1)}, u32[]{:S(2)}) copy-start(bf16[512,1024]{0,1:T(8,128)(2,1)} %copy.40) | copy-start | bytes 3145732
  32.0 11.8 %copy-start.5 = (bf16[512,1024]{0,1:T(8,128)(2,1)S(1)}, bf16[512,1024]{0,1:T(8,128)(2,1)}, u32[]{:S(2)}) copy-start(bf16[512,1024]{0,1:T(8,128)(2,1)} %copy.41) | copy-start | bytes 3145732
  32.0 11.8 %copy-start.6 = (bf16[512,1024]{0,1:T(8,128)(2,1)S(1)}, bf16[512,1024]{0,1:T(8,128)(2,1)}, u32[]{:S(2)}) copy-start(bf16[512,1024]{0,1:T(8,128)(2,1)} %copy.42) | copy-start | bytes 3145732
  32.9 19.5 %collective-permute-start.6 = (bf16[64,4096]{1,0:T(8,128)(2,1)}, bf16[64,4096]{1,0:T(8,128)(2,1)S(1)}, u32[]{:S(2)}, u32[]{:S(2)}) collective-permute-start(bf16[64,4096]{1,0:T(8,128)(2,1)} %pad_maximum_fusion.9), channel_id=1, source_target_pairs={{0,8},{1,9},{2,10},{3,11},{4,12},{5,13},{6,14},{7,15},{8,0},{9,1},... | collective-permute-start | bytes 1572872 | tf_op jit(solution)/shard_map/ppermute | solution.py:195
  42.3 43.6 %collective-permute-start.2 = (bf16[128,4096]{1,0:T(8,128)(2,1)}, bf16[128,4096]{1,0:T(8,128)(2,1)S(1)}, u32[]{:S(2)}, u32[]{:S(2)}) collective-permute-start(bf16[128,4096]{1,0:T(8,128)(2,1)} %pad_maximum_fusion.4), channel_id=1, source_target_pairs={{0,4},{1,5},{2,6},{3,7},{4,0},{5,1},{6,2},{7,3},{8,12},{9,13},{10,... | collective-permute-start | bytes 3145736 | tf_op jit(solution)/shard_map/ppermute | solution.py:195
  45.6 103.5 %all-to-all-start = ((bf16[8,512,384]{1,2,0:T(8,128)(2,1)}), bf16[8,512,384]{1,2,0:T(8,128)(2,1)}, u32[]{:S(2)}, u32[]{:S(2)}) async-start(bf16[8,512,384]{1,2,0:T(8,128)(2,1)} %pad_maximum_fusion), calls=%async_computation | async-start | bytes 6291456 | tf_op jit(solution)/shard_map/all_to_all | solution.py:250
  52.4 36.9 %collective-permute-start.7 = (bf16[128,4096]{1,0:T(8,128)(2,1)S(1)}, bf16[128,4096]{1,0:T(8,128)(2,1)S(1)}, u32[]{:S(2)}, u32[]{:S(2)}) collective-permute-start(bf16[128,4096]{1,0:T(8,128)(2,1)S(1)} %pad_maximum_fusion.5), channel_id=1, source_target_pairs={{0,2},{1,3},{2,0},{3,1},{4,6},{5,7},{6,4},{7,5},{8,10},{9,11},{10,... | collective-permute-start | bytes 3145736 | tf_op jit(solution)/shard_map/ppermute | solution.py:195
  87.1 45.6 %collective-permute-start.3 = (bf16[256,4096]{1,0:T(8,128)(2,1)S(1)}, bf16[256,4096]{1,0:T(8,128)(2,1)S(1)}, u32[]{:S(2)}, u32[]{:S(2)}) collective-permute-start(bf16[256,4096]{1,0:T(8,128)(2,1)S(1)} %pad_maximum_fusion.1), channel_id=1, source_target_pairs={{0,2},{1,3},{2,0},{3,1},{4,6},{5,7},{6,4},{7,5},{8,10},{9,11},{10,... | collective-permute-start | bytes 6291464 | tf_op jit(solution)/shard_map/ppermute | solution.py:195
  89.6 56.5 %collective-permute-start.8 = (bf16[256,4096]{1,0:T(8,128)(2,1)S(1)}, bf16[256,4096]{1,0:T(8,128)(2,1)S(1)}, u32[]{:S(2)}, u32[]{:S(2)}) collective-permute-start(bf16[256,4096]{1,0:T(8,128)(2,1)S(1)} %pad_maximum_fusion.2), channel_id=1, source_target_pairs={{0,4},{1,5},{2,6},{3,7},{4,0},{5,1},{6,2},{7,3},{8,12},{9,13},{10,... | collective-permute-start | bytes 6291464 | tf_op jit(solution)/shard_map/ppermute | solution.py:195
  134.2 35.7 %collective-permute-start.4 = (bf16[512,4096]{1,0:T(8,128)(2,1)}, bf16[512,4096]{1,0:T(8,128)(2,1)}, u32[]{:S(2)}, u32[]{:S(2)}) collective-permute-start(bf16[512,4096]{1,0:T(8,128)(2,1)} %constant_dynamic-update-slice_fusion.1), channel_id=1, source_target_pairs={{0,1},{1,0},{2,3},{3,2},{4,5},{5,4},{6,7},{7,6},{8,9},{9,8},{10,11... | collective-permute-start | bytes 12582920 | tf_op jit(solution)/shard_map/ppermute | solution.py:195
  147.7 26.8 %collective-permute-start.9 = (bf16[512,4096]{1,0:T(8,128)(2,1)}, bf16[512,4096]{1,0:T(8,128)(2,1)}, u32[]{:S(2)}, u32[]{:S(2)}) collective-permute-start(bf16[512,4096]{1,0:T(8,128)(2,1)} %constant_dynamic-update-slice_fusion.6), channel_id=1, source_target_pairs={{0,1},{1,0},{2,3},{3,2},{4,5},{5,4},{6,7},{7,6},{8,9},{9,8},{10,11... | collective-permute-start | bytes 12582920 | tf_op jit(solution)/shard_map/ppermute | solution.py:195
  149.1 36.0 %all-to-all-start.2 = ((bf16[8,256,128]{2,1,0:T(8,128)(2,1)}), bf16[8,256,128]{2,1,0:T(8,128)(2,1)S(1)}, u32[]{:S(2)}, u32[]{:S(2)}) async-start(bf16[8,256,128]{2,1,0:T(8,128)(2,1)} %bitcast_bitcast_fusion), calls=%async_computation.2 | async-start | bytes 1048576 | tf_op jit(solution)/shard_map/all_to_all | solution.py:251
  193.5 51.5 %all-to-all-start.1 = ((bf16[8,256,128]{2,1,0:T(8,128)(2,1)}), bf16[8,256,128]{2,1,0:T(8,128)(2,1)}, u32[]{:S(2)}, u32[]{:S(2)}) async-start(bf16[8,256,128]{2,1,0:T(8,128)(2,1)} %bitcast.16), calls=%async_computation.1 | async-start | bytes 1048576 | tf_op jit(solution)/shard_map/all_to_all | solution.py:266
  214.3 36.7 %collective-permute-start.11 = (bf16[2048,1024]{1,0:T(8,128)(2,1)}, bf16[2048,1024]{1,0:T(8,128)(2,1)}, u32[]{:S(2)}, u32[]{:S(2)}) collective-permute-start(bf16[2048,1024]{1,0:T(8,128)(2,1)} %convolution_convert_fusion), channel_id=1, source_target_pairs={{0,1},{1,0},{2,3},{3,2},{4,5},{5,4},{6,7},{7,6},{8,9},{9,8},{10,11... | collective-permute-start | bytes 12582920 | tf_op jit(solution)/shard_map/ppermute | solution.py:195
  218.6 43.9 %collective-permute-start.10 = (bf16[2048,1024]{1,0:T(8,128)(2,1)}, bf16[2048,1024]{1,0:T(8,128)(2,1)}, u32[]{:S(2)}, u32[]{:S(2)}) collective-permute-start(bf16[2048,1024]{1,0:T(8,128)(2,1)} %convolution_convert_fusion.1), channel_id=1, source_target_pairs={{0,1},{1,0},{2,3},{3,2},{4,5},{5,4},{6,7},{7,6},{8,9},{9,8},{10,11... | collective-permute-start | bytes 12582920 | tf_op jit(solution)/shard_map/ppermute | solution.py:195
  245.0 130.9 %all-to-all-start.3 = ((bf16[8,512,384]{2,1,0:T(8,128)(2,1)}), bf16[8,512,384]{2,1,0:T(8,128)(2,1)S(1)}, u32[]{:S(2)}, u32[]{:S(2)}) async-start(bf16[8,512,384]{2,1,0:T(8,128)(2,1)} %bitcast.36), calls=%async_computation.3 | async-start | bytes 6291456 | tf_op jit(solution)/shard_map/all_to_all | solution.py:304
  257.9 56.4 %collective-permute-start.12 = (bf16[1024,1024]{1,0:T(8,128)(2,1)}, bf16[1024,1024]{1,0:T(8,128)(2,1)}, u32[]{:S(2)}, u32[]{:S(2)}) collective-permute-start(bf16[1024,1024]{1,0:T(8,128)(2,1)} %slice.131), channel_id=1, source_target_pairs={{0,2},{1,3},{2,0},{3,1},{4,6},{5,7},{6,4},{7,5},{8,10},{9,11},{10,... | collective-permute-start | bytes 6291464 | tf_op jit(solution)/shard_map/ppermute | solution.py:195
  260.5 49.8 %collective-permute-start.17 = (bf16[512,1024]{1,0:T(8,128)(2,1)}, bf16[512,1024]{1,0:T(8,128)(2,1)}, u32[]{:S(2)}, u32[]{:S(2)}) collective-permute-start(bf16[512,1024]{1,0:T(8,128)(2,1)} %slice.141), channel_id=1, source_target_pairs={{0,4},{1,5},{2,6},{3,7},{4,0},{5,1},{6,2},{7,3},{8,12},{9,13},{10,... | collective-permute-start | bytes 3145736 | tf_op jit(solution)/shard_map/ppermute | solution.py:195
  267.9 64.7 %collective-permute-start.16 = (bf16[512,1024]{1,0:T(8,128)(2,1)S(1)}, bf16[512,1024]{1,0:T(8,128)(2,1)S(1)}, u32[]{:S(2)}, u32[]{:S(2)}) collective-permute-start(bf16[512,1024]{1,0:T(8,128)(2,1)S(1)} %slice.139), channel_id=1, source_target_pairs={{0,4},{1,5},{2,6},{3,7},{4,0},{5,1},{6,2},{7,3},{8,12},{9,13},{10,... | collective-permute-start | bytes 3145736 | tf_op jit(solution)/shard_map/ppermute | solution.py:195
  312.2 24.3 %collective-permute-start.18 = (bf16[512,1024]{1,0:T(8,128)(2,1)S(1)}, bf16[512,1024]{1,0:T(8,128)(2,1)S(1)}, u32[]{:S(2)}, u32[]{:S(2)}) collective-permute-start(bf16[512,1024]{1,0:T(8,128)(2,1)S(1)} %add_convert_fusion.5), channel_id=1, source_target_pairs={{0,2},{1,3},{2,0},{3,1},{4,6},{5,7},{6,4},{7,5},{8,10},{9,11},{10,... | collective-permute-start | bytes 3145736 | tf_op jit(solution)/shard_map/ppermute | solution.py:195
  317.0 37.6 %collective-permute-start.13 = (bf16[512,1024]{1,0:T(8,128)(2,1)S(1)}, bf16[512,1024]{1,0:T(8,128)(2,1)S(1)}, u32[]{:S(2)}, u32[]{:S(2)}) collective-permute-start(bf16[512,1024]{1,0:T(8,128)(2,1)S(1)} %slice.133), channel_id=1, source_target_pairs={{0,4},{1,5},{2,6},{3,7},{4,0},{5,1},{6,2},{7,3},{8,12},{9,13},{10,... | collective-permute-start | bytes 3145736 | tf_op jit(solution)/shard_map/ppermute | solution.py:195
  337.2 21.3 %collective-permute-start.19 = (bf16[256,1024]{1,0:T(8,128)(2,1)S(1)}, bf16[256,1024]{1,0:T(8,128)(2,1)S(1)}, u32[]{:S(2)}, u32[]{:S(2)}) collective-permute-start(bf16[256,1024]{1,0:T(8,128)(2,1)S(1)} %slice.143), channel_id=1, source_target_pairs={{0,8},{1,9},{2,10},{3,11},{4,12},{5,13},{6,14},{7,15},{8,0},{9,1},... | collective-permute-start | bytes 1572872 | tf_op jit(solution)/shard_map/ppermute | solution.py:195
  355.1 19.1 %collective-permute-start.14 = (bf16[256,1024]{1,0:T(8,128)(2,1)S(1)}, bf16[256,1024]{1,0:T(8,128)(2,1)S(1)}, u32[]{:S(2)}, u32[]{:S(2)}) collective-permute-start(bf16[256,1024]{1,0:T(8,128)(2,1)S(1)} %slice.135), channel_id=1, source_target_pairs={{0,8},{1,9},{2,10},{3,11},{4,12},{5,13},{6,14},{7,15},{8,0},{9,1},... | collective-permute-start | bytes 1572872 | tf_op jit(solution)/shard_map/ppermute | solution.py:195
  358.7 16.5 %copy-start.10 = (bf16[256,1024]{1,0:T(8,128)(2,1)}, bf16[256,1024]{1,0:T(8,128)(2,1)S(1)}, u32[]{:S(2)}) copy-start(bf16[256,1024]{1,0:T(8,128)(2,1)S(1)} %add_convert_fusion.8) | copy-start | bytes 1572868
  359.5 21.0 %collective-permute-start.20 = (bf16[128,1024]{1,0:T(8,128)(2,1)}, bf16[128,1024]{1,0:T(8,128)(2,1)S(1)}, u32[]{:S(2)}, u32[]{:S(2)}) collective-permute-start(bf16[128,1024]{1,0:T(8,128)(2,1)} %slice.145), channel_id=1, source_target_pairs={{0,16},{1,17},{2,18},{3,19},{4,20},{5,21},{6,22},{7,23},{8,24},{9,... | collective-permute-start | bytes 786440 | tf_op jit(solution)/shard_map/ppermute | solution.py:195
  375.3 12.7 %collective-permute-start.15 = (bf16[128,1024]{1,0:T(8,128)(2,1)}, bf16[128,1024]{1,0:T(8,128)(2,1)}, u32[]{:S(2)}, u32[]{:S(2)}) collective-permute-start(bf16[128,1024]{1,0:T(8,128)(2,1)} %slice.137), channel_id=1, source_target_pairs={{0,16},{1,17},{2,18},{3,19},{4,20},{5,21},{6,22},{7,23},{8,24},{9,... | collective-permute-start | bytes 786440 | tf_op jit(solution)/shard_map/ppermute | solution.py:195
  378.0 11.9 %copy-start.1 = (bf16[256,1024]{1,0:T(8,128)(2,1)S(1)}, bf16[256,1024]{1,0:T(8,128)(2,1)}, u32[]{:S(2)}) copy-start(bf16[256,1024]{1,0:T(8,128)(2,1)} %param.9) | copy-start | bytes 1572868
  (11 other events, 46.4 us)
